TPU v7x, 128 devices: a whole 4x4x4 slice. The times are simulated.
128 devices in a mesh: seq: 16 (over z, y_lo, core), chan: 8 (over y_hi, x).
Axes of the slice: x: 4, y: 4 (y_hi: 2, y_lo: 2; y = y_hi * 2 + y_lo), z: 4, core: 2. Of those that a mesh axis runs over, the one named last changes fastest.
Arguments:
- inputs: bfloat16 [16384, 4096], P('seq', 'chan'), may hold values from -6 to 6
- out_grad: bfloat16 [16384, 4096], P('seq', 'chan'), may hold values from -6 to 6
- out_weight: bfloat16 [4096, 4096], P('chan'), may hold values from -0.09375 to 0.09375
- filt: float32 [2048, 4096], P('seq', 'chan'), may hold values from -1.2 to 1.2
Outputs:
- grad_in: bfloat16 [16384, 4096], P('seq', 'chan')
- filt_grad: float32 [2048, 4096], P('seq', 'chan')
All inputs are finite; a program needn't handle non-finite values.
Results may differ from a plain program's by a relative error of at most 0.0049.
Values may be sent and summed in bfloat16 or wider, within the bound.
A program may use at most 256 MiB of HBM per device.

v0:
```python
import math
import jax
import jax.numpy as jnp
from jax import lax
from jax.sharding import PartitionSpec as P

LAG_STEPS = 2
BLOCK = 256
highest = lax.Precision.HIGHEST
higher = lax.Precision.HIGH


def from_behind(block, axis, distance):
    devices = range(lax.axis_size(axis))
    route = [(i - distance, i) for i in devices if i - distance in devices]
    return lax.ppermute(block, axis, route)


def per_device(inputs, out_grad, out_weight, filt):
    span_len, chan_width = inputs.shape
    block_len = BLOCK
    frame_len = 2 * BLOCK
    mixed_sum = lax.dot_general(
        lax.all_gather(out_grad, "chan", axis=1, tiled=True),
        out_weight,
        (((1,), (1,)), ((), ())),
        preferred_element_type=jnp.float32,
    )
    grad_mix = mixed_sum.astype(jnp.bfloat16)
    whole_filter = lax.all_gather(filt, "seq", axis=0, tiled=True)
    later_list = [from_behind(grad_mix, "seq", -offset) for offset in range(1, LAG_STEPS + 1)]
    extended = jnp.concatenate([grad_mix] + later_list, axis=0)
    freq_index = lax.iota(jnp.int32, frame_len)[:, None]
    time_index = lax.iota(jnp.int32, block_len)[None, :]
    angles = (freq_index * time_index % frame_len).astype(jnp.float32) * (2.0 * math.pi / frame_len)
    cos_table = jnp.cos(angles)
    sin_table = jnp.sin(angles)
    parity = jnp.where(lax.iota(jnp.int32, frame_len) % 2 == 0, 1.0, -1.0).astype(jnp.float32)[
        None, :, None
    ]

    def spectrum(blocks, level):
        real_part = jnp.einsum("fb,nbc->nfc", cos_table, blocks, precision=level)
        imag_part = -jnp.einsum("fb,nbc->nfc", sin_table, blocks, precision=level)
        return (real_part, imag_part)

    def inverse(real_part, imag_part):
        front = jnp.einsum("fa,nfc->nac", cos_table, real_part, precision=highest)
        back = jnp.einsum("fa,nfc->nac", sin_table, imag_part, precision=highest)
        return (front - back) / frame_len

    base_real, base_imag = spectrum(
        extended.astype(jnp.float32).reshape(-1, block_len, chan_width), higher
    )
    win_real = base_real[:-1] + parity * base_real[1:]
    win_imag = base_imag[:-1] + parity * base_imag[1:]
    lag_real, lag_imag = spectrum(whole_filter.reshape(-1, block_len, chan_width), highest)
    val_real, val_imag = spectrum(
        inputs.astype(jnp.float32).reshape(-1, block_len, chan_width), higher
    )
    lag_count = lag_real.shape[0]
    block_count = val_real.shape[0]

    def add_lag(lag_index, totals):
        slice_real = lax.dynamic_slice_in_dim(win_real, lag_index, block_count, 0)
        slice_imag = lax.dynamic_slice_in_dim(win_imag, lag_index, block_count, 0)
        coef_real = lax.dynamic_index_in_dim(lag_real, lag_index, 0, keepdims=False)
        coef_imag = lax.dynamic_index_in_dim(lag_imag, lag_index, 0, keepdims=False)
        return (
            totals[0] + coef_real * slice_real + coef_imag * slice_imag,
            totals[1] + coef_real * slice_imag - coef_imag * slice_real,
        )

    empty_in = jnp.zeros((block_count, frame_len, chan_width), jnp.float32)
    sum_real, sum_imag = lax.fori_loop(0, lag_count, add_lag, (empty_in, empty_in))

    def add_block(block_index, totals):
        slice_real = lax.dynamic_slice_in_dim(win_real, block_index, lag_count, 0)
        slice_imag = lax.dynamic_slice_in_dim(win_imag, block_index, lag_count, 0)
        coef_real = lax.dynamic_index_in_dim(val_real, block_index, 0, keepdims=False)
        coef_imag = lax.dynamic_index_in_dim(val_imag, block_index, 0, keepdims=False)
        return (
            totals[0] + coef_real * slice_real + coef_imag * slice_imag,
            totals[1] + coef_real * slice_imag - coef_imag * slice_real,
        )

    empty_lag = jnp.zeros((lag_count, frame_len, chan_width), jnp.float32)
    grad_real, grad_imag = lax.fori_loop(0, block_count, add_block, (empty_lag, empty_lag))
    grad_in = inverse(sum_real, sum_imag).reshape(span_len, chan_width).astype(jnp.bfloat16)
    local_grad = inverse(grad_real, grad_imag).reshape(-1, chan_width)
    seq_count = lax.axis_size("seq")
    grad_scale = 1.0 / math.sqrt(span_len * seq_count)
    owned = lax.psum_scatter(local_grad, "seq", scatter_dimension=0, tiled=True)
    filt_grad = owned * grad_scale
    return (grad_in, filt_grad)


def solution(mesh):
    in_specs = (P("seq", "chan"), P("seq", "chan"), P("chan", None), P("seq", "chan"))
    out_specs = (P("seq", "chan"), P("seq", "chan"))
    return jax.shard_map(
        per_device, mesh=mesh, in_specs=in_specs, out_specs=out_specs, check_vma=False
    )
```

profile of v0, /device:TPU:3, one launch (start us, length us, event | category | flops | bytes accessed | tf_op | source)
XLA Modules:
  0.0 510.7 jit_solution(2675074448289331453)
XLA Ops:
  8.7 123.2 %all-gather.5.cloned.1.call-done = bf16[1024,4096]{1,0:T(8,128)(2,1)} async-done(((bf16[1024,512]{1,0:T(8,128)(2,1)}), bf16[1024,4096]{1,0:T(8,128)(2,1)}) %all-gather.5.cloned.1.call-update) | async-done | bytes 8388624 | tf_op jit(solution)/shard_map/all_gather | solution.py:24
  131.9 9.1 %convolution_convert_fusion = bf16[1024,512]{1,0:T(8,128)(2,1)S(1)} fusion(bf16[1024,4096]{1,0:T(8,128)(2,1)} %all-gather.5.cloned.1.call-done, bf16[512,4096]{1,0:T(8,128)(2,1)} %param.10), kind=kOutput, calls=%fused_computation.25 | convolution fusion | flops 4295491584 | bytes 13631488 | tf_op jit(solution)/shard_map/dot_general | solution.py:23
  141.0 3.4 collective-permute-start
  146.0 4.7 convolution_bitcast_fusion.2
  150.7 4.7 negate_bitcast_fusion.2
  155.5 51.2 %all-gather.3.cloned.1.call-done = f32[2048,512]{1,0:T(8,128)} async-done(((f32[128,512]{1,0:T(8,128)}), f32[2048,512]{1,0:T(8,128)}) %all-gather.3.cloned.1.call-update) | async-done | bytes 4194320 | tf_op jit(solution)/shard_map/all_gather | solution.py:30
  206.6 14.5 %convolution_bitcast_fusion.1 = f32[8,512,512]{2,1,0:T(8,128)} fusion(f32[8,256,512]{2,1,0:T(8,128)} %bitcast.77), kind=kOutput, calls=%fused_computation.21 | convolution fusion | flops 6444285952 | bytes 12582912 | tf_op jit(solution)/shard_map/fb,nbc->nfc/dot_general | solution.py:43
  222.7 5.7 %convolution_bitcast_fusion = f32[12,512,512]{1,2,0:T(8,128)S(1)} fusion(bf16[12,256,512]{2,1,0:T(8,128)(2,1)S(1)} %bitcast.75), kind=kOutput, calls=%fused_computation.18 | convolution fusion | flops 4833673216 | bytes 15728640 | tf_op jit(solution)/shard_map/fb,nbc->nfc/dot_general | solution.py:43
  228.4 9.9 %negate_bitcast_fusion = f32[12,512,512]{1,2,0:T(8,128)} fusion(bf16[12,256,512]{2,1,0:T(8,128)(2,1)S(1)} %bitcast.76), kind=kOutput, calls=%fused_computation.12 | convolution fusion | flops 4836818944 | bytes 15728640 | tf_op jit(solution)/shard_map/fb,nbc->nfc/dot_general | solution.py:44
  238.3 16.4 %fusion.4 = (f32[11,512,512]{1,2,0:T(8,128)}, f32[11,512,512]{1,2,0:T(8,128)}) fusion(f32[12,512,512]{1,2,0:T(8,128)} %negate_bitcast_fusion, f32[512]{0:T(512)S(1)} %fusion.39, f32[12,512,512]{1,2,0:T(8,128)S(1)} %convolution_bitcast_fusion), kind=kLoop, calls=%fused_computation.14 | loop fusion | flops 11534336 | bytes 69208064 | tf_op jit(solution)/shard_map/add | solution.py:56
  254.7 12.1 %copy.12 = f32[11,512,512]{2,1,0:T(8,128)} copy(f32[11,512,512]{1,2,0:T(8,128)} %get-tuple-element.355) | data formatting | bytes 23068672
  266.8 12.1 %copy.13 = f32[11,512,512]{2,1,0:T(8,128)} copy(f32[11,512,512]{1,2,0:T(8,128)} %get-tuple-element.354) | data formatting | bytes 23068672
  279.0 77.0 %while.33 = (s32[]{:T(128)}, f32[8,512,512]{2,1,0:T(8,128)}, f32[8,512,512]{2,1,0:T(8,128)}, f32[4,512,512]{2,1,0:T(8,128)}, f32[11,512,512]{2,1,0:T(8,128)}, /*...) while((s32[]{:T(128)}, f32[8,512,512]{2,1,0:T(8,128)}, ...), condition=%wide.region_3.4_spmd.clone, body=%wide.region_2.3_spmd.clone.sunk | while | flops 20971524 | bytes 56623212 | solution.py:88
  281.1 11.9 %fusion.96 = (f32[8,512,512]{2,1,0:T(8,128)}, f32[8,512,512]{2,1,0:T(8,128)}) fusion(f32[8,512,512]{2,1,0:T(8,128)} %get-tuple-element.496, f32[11,512,512]{2,1,0:T(8,128)} %get-tuple-element.509, s32[]{:T(128)} %get-tuple-element.494, f32[11,512,512]{2,1,0:T(8,128)} %get-tuple-element.507, f32[512,512]{1,0:T(8,128)S(1)} %get-tuple-element.454, ...), kind=kLoop, calls=%fused_computation.7.clone.1 | loop fusion | flops 20971520 | bytes 52428804 | tf_op jit(solution)/shard_map/while/body/eval_jaxpr/sub | solution.py:84
  294.7 19.3 %fusion.96 = (f32[8,512,512]{2,1,0:T(8,128)}, f32[8,512,512]{2,1,0:T(8,128)}) fusion(f32[8,512,512]{2,1,0:T(8,128)} %get-tuple-element.496, f32[11,512,512]{2,1,0:T(8,128)} %get-tuple-element.509, s32[]{:T(128)} %get-tuple-element.494, f32[11,512,512]{2,1,0:T(8,128)} %get-tuple-element.507, f32[512,512]{1,0:T(8,128)S(1)} %get-tuple-element.454, ...), kind=kLoop, calls=%fused_computation.7.clone.1 | loop fusion | flops 20971520 | bytes 52428804 | tf_op jit(solution)/shard_map/while/body/eval_jaxpr/sub | solution.py:84
  315.7 19.3 %fusion.96 = (f32[8,512,512]{2,1,0:T(8,128)}, f32[8,512,512]{2,1,0:T(8,128)}) fusion(f32[8,512,512]{2,1,0:T(8,128)} %get-tuple-element.496, f32[11,512,512]{2,1,0:T(8,128)} %get-tuple-element.509, s32[]{:T(128)} %get-tuple-element.494, f32[11,512,512]{2,1,0:T(8,128)} %get-tuple-element.507, f32[512,512]{1,0:T(8,128)S(1)} %get-tuple-element.454, ...), kind=kLoop, calls=%fused_computation.7.clone.1 | loop fusion | flops 20971520 | bytes 52428804 | tf_op jit(solution)/shard_map/while/body/eval_jaxpr/sub | solution.py:84
  336.7 19.3 %fusion.96 = (f32[8,512,512]{2,1,0:T(8,128)}, f32[8,512,512]{2,1,0:T(8,128)}) fusion(f32[8,512,512]{2,1,0:T(8,128)} %get-tuple-element.496, f32[11,512,512]{2,1,0:T(8,128)} %get-tuple-element.509, s32[]{:T(128)} %get-tuple-element.494, f32[11,512,512]{2,1,0:T(8,128)} %get-tuple-element.507, f32[512,512]{1,0:T(8,128)S(1)} %get-tuple-element.454, ...), kind=kLoop, calls=%fused_computation.7.clone.1 | loop fusion | flops 20971520 | bytes 52428804 | tf_op jit(solution)/shard_map/while/body/eval_jaxpr/sub | solution.py:84
  356.0 14.5 %fusion.15 = f32[8,512,256]{1,2,0:T(8,128)S(1)} fusion(f32[8,512,512]{2,1,0:T(8,128)} %get-tuple-element.254), kind=kOutput, calls=%fused_computation.38 | convolution fusion | flops 6444285952 | bytes 12582912 | tf_op jit(solution)/shard_map/fa,nfc->nac/dot_general | solution.py:48
  370.5 13.7 %subtract_multiply_fusion = f32[8,512,256]{1,2,0:T(8,128)} fusion(f32[8,512,256]{1,2,0:T(8,128)S(1)} %fusion.15, f32[8,512,512]{2,1,0:T(8,128)S(1)} %copy-done.2), kind=kOutput, calls=%fused_computation.19 | convolution fusion | flops 6446383104 | bytes 16777216 | tf_op jit(solution)/shard_map/fa,nfc->nac/dot_general | solution.py:49
  384.3 14.6 %negate_bitcast_fusion.1 = f32[8,512,512]{2,1,0:T(8,128)} fusion(f32[8,256,512]{2,1,0:T(8,128)} %bitcast.78), kind=kOutput, calls=%fused_computation.17 | convolution fusion | flops 6446383104 | bytes 12582912 | tf_op jit(solution)/shard_map/fb,nbc->nfc/dot_general | solution.py:44
  398.9 88.1 %while.32 = (s32[]{:T(128)}, f32[4,512,512]{2,1,0:T(8,128)}, f32[4,512,512]{2,1,0:T(8,128)}, f32[8,512,512]{2,1,0:T(8,128)}, f32[11,512,512]{2,1,0:T(8,128)}, /*...) while((s32[]{:T(128)}, f32[4,512,512]{2,1,0:T(8,128)}, ...), condition=%wide.region_1.2_spmd.clone, body=%wide.region_0.1_spmd.clone.sunk | while | flops 10485763 | bytes 31457388 | solution.py:75
  400.6 6.9 %fusion.95 = (f32[4,512,512]{2,1,0:T(8,128)}, f32[4,512,512]{2,1,0:T(8,128)}) fusion(f32[4,512,512]{2,1,0:T(8,128)} %get-tuple-element.469, f32[11,512,512]{2,1,0:T(8,128)} %get-tuple-element.482, s32[]{:T(128)} %get-tuple-element.467, f32[11,512,512]{2,1,0:T(8,128)} %get-tuple-element.480, f32[512,512]{1,0:T(8,128)S(1)} %get-tuple-element.443, ...), kind=kLoop, calls=%fused_computation.1.clone.1 | loop fusion | flops 10485760 | bytes 27262980 | tf_op jit(solution)/shard_map/while/body/eval_jaxpr/sub | solution.py:71
  407.5 1.7 dynamic-slice_bitcast_fusion.6
  409.3 9.6 %fusion.95 = (f32[4,512,512]{2,1,0:T(8,128)}, f32[4,512,512]{2,1,0:T(8,128)}) fusion(f32[4,512,512]{2,1,0:T(8,128)} %get-tuple-element.469, f32[11,512,512]{2,1,0:T(8,128)} %get-tuple-element.482, s32[]{:T(128)} %get-tuple-element.467, f32[11,512,512]{2,1,0:T(8,128)} %get-tuple-element.480, f32[512,512]{1,0:T(8,128)S(1)} %get-tuple-element.443, ...), kind=kLoop, calls=%fused_computation.1.clone.1 | loop fusion | flops 10485760 | bytes 27262980 | tf_op jit(solution)/shard_map/while/body/eval_jaxpr/sub | solution.py:71
  420.7 9.7 %fusion.95 = (f32[4,512,512]{2,1,0:T(8,128)}, f32[4,512,512]{2,1,0:T(8,128)}) fusion(f32[4,512,512]{2,1,0:T(8,128)} %get-tuple-element.469, f32[11,512,512]{2,1,0:T(8,128)} %get-tuple-element.482, s32[]{:T(128)} %get-tuple-element.467, f32[11,512,512]{2,1,0:T(8,128)} %get-tuple-element.480, f32[512,512]{1,0:T(8,128)S(1)} %get-tuple-element.443, ...), kind=kLoop, calls=%fused_computation.1.clone.1 | loop fusion | flops 10485760 | bytes 27262980 | tf_op jit(solution)/shard_map/while/body/eval_jaxpr/sub | solution.py:71
  432.2 9.7 %fusion.95 = (f32[4,512,512]{2,1,0:T(8,128)}, f32[4,512,512]{2,1,0:T(8,128)}) fusion(f32[4,512,512]{2,1,0:T(8,128)} %get-tuple-element.469, f32[11,512,512]{2,1,0:T(8,128)} %get-tuple-element.482, s32[]{:T(128)} %get-tuple-element.467, f32[11,512,512]{2,1,0:T(8,128)} %get-tuple-element.480, f32[512,512]{1,0:T(8,128)S(1)} %get-tuple-element.443, ...), kind=kLoop, calls=%fused_computation.1.clone.1 | loop fusion | flops 10485760 | bytes 27262980 | tf_op jit(solution)/shard_map/while/body/eval_jaxpr/sub | solution.py:71
  443.6 9.7 %fusion.95 = (f32[4,512,512]{2,1,0:T(8,128)}, f32[4,512,512]{2,1,0:T(8,128)}) fusion(f32[4,512,512]{2,1,0:T(8,128)} %get-tuple-element.469, f32[11,512,512]{2,1,0:T(8,128)} %get-tuple-element.482, s32[]{:T(128)} %get-tuple-element.467, f32[11,512,512]{2,1,0:T(8,128)} %get-tuple-element.480, f32[512,512]{1,0:T(8,128)S(1)} %get-tuple-element.443, ...), kind=kLoop, calls=%fused_computation.1.clone.1 | loop fusion | flops 10485760 | bytes 27262980 | tf_op jit(solution)/shard_map/while/body/eval_jaxpr/sub | solution.py:71
  455.0 9.4 %fusion.95 = (f32[4,512,512]{2,1,0:T(8,128)}, f32[4,512,512]{2,1,0:T(8,128)}) fusion(f32[4,512,512]{2,1,0:T(8,128)} %get-tuple-element.469, f32[11,512,512]{2,1,0:T(8,128)} %get-tuple-element.482, s32[]{:T(128)} %get-tuple-element.467, f32[11,512,512]{2,1,0:T(8,128)} %get-tuple-element.480, f32[512,512]{1,0:T(8,128)S(1)} %get-tuple-element.443, ...), kind=kLoop, calls=%fused_computation.1.clone.1 | loop fusion | flops 10485760 | bytes 27262980 | tf_op jit(solution)/shard_map/while/body/eval_jaxpr/sub | solution.py:71
  466.2 9.4 %fusion.95 = (f32[4,512,512]{2,1,0:T(8,128)}, f32[4,512,512]{2,1,0:T(8,128)}) fusion(f32[4,512,512]{2,1,0:T(8,128)} %get-tuple-element.469, f32[11,512,512]{2,1,0:T(8,128)} %get-tuple-element.482, s32[]{:T(128)} %get-tuple-element.467, f32[11,512,512]{2,1,0:T(8,128)} %get-tuple-element.480, f32[512,512]{1,0:T(8,128)S(1)} %get-tuple-element.443, ...), kind=kLoop, calls=%fused_computation.1.clone.1 | loop fusion | flops 10485760 | bytes 27262980 | tf_op jit(solution)/shard_map/while/body/eval_jaxpr/sub | solution.py:71
  477.4 9.4 %fusion.95 = (f32[4,512,512]{2,1,0:T(8,128)}, f32[4,512,512]{2,1,0:T(8,128)}) fusion(f32[4,512,512]{2,1,0:T(8,128)} %get-tuple-element.469, f32[11,512,512]{2,1,0:T(8,128)} %get-tuple-element.482, s32[]{:T(128)} %get-tuple-element.467, f32[11,512,512]{2,1,0:T(8,128)} %get-tuple-element.480, f32[512,512]{1,0:T(8,128)S(1)} %get-tuple-element.443, ...), kind=kLoop, calls=%fused_computation.1.clone.1 | loop fusion | flops 10485760 | bytes 27262980 | tf_op jit(solution)/shard_map/while/body/eval_jaxpr/sub | solution.py:71
  487.0 8.2 %fusion.17 = f32[4,512,256]{1,2,0:T(8,128)S(1)} fusion(f32[4,512,512]{2,1,0:T(8,128)} %get-tuple-element.252), kind=kOutput, calls=%fused_computation.40 | convolution fusion | flops 3223060480 | bytes 6291456 | tf_op jit(solution)/shard_map/fa,nfc->nac/dot_general | solution.py:48
  495.2 7.0 %multiply_convert_fusion = bf16[4,512,256]{1,2,0:T(8,128)(2,1)} fusion(f32[4,512,256]{1,2,0:T(8,128)S(1)} %fusion.17, f32[4,512,512]{2,1,0:T(8,128)S(1)} %copy-done.3), kind=kOutput, calls=%fused_computation.24 | convolution fusion | flops 3224633344 | bytes 7340032 | tf_op jit(solution)/shard_map/fa,nfc->nac/dot_general | solution.py:49
  (36 shorter events, 25.1 us)
Async XLA Ops:
  7.2 138.8 %copy-start = (bf16[1024,512]{1,0:T(8,128)(2,1)S(1)}, bf16[1024,512]{1,0:T(8,128)(2,1)}, u32[]{:S(2)}) copy-start(bf16[1024,512]{1,0:T(8,128)(2,1)} %param.8) | copy-start | bytes 3145732
  7.2 124.8 %all-gather.5.cloned.1.call-start = ((), (), s32[]{:S(2)}) async-start(), calls=%async_computation.2 | async-start | bytes 9437184 | tf_op jit(solution)/shard_map/all_gather | solution.py:24
  7.9 198.7 %all-gather.3.cloned.1.call-start = ((), (), s32[]{:S(2)}) async-start(), calls=%async_computation.1 | async-start | bytes 4456448 | tf_op jit(solution)/shard_map/all_gather | solution.py:30
  8.7 493.6 %reduce-scatter.2.cloned.1.call-start = ((), (), s32[]{:S(2)}) async-start(), calls=%async_computation.3 | async-start | bytes 4456448 | tf_op jit(solution)/shard_map/reduce_scatter | solution.py:93
  141.0 80.1 %collective-permute-start = (bf16[1024,512]{1,0:T(8,128)(2,1)S(1)}, bf16[1024,512]{1,0:T(8,128)(2,1)S(1)}, u32[]{:S(2)}, u32[]{:S(2)}) collective-permute-start(bf16[1024,512]{1,0:T(8,128)(2,1)S(1)} %convolution_convert_fusion), channel_id=1, source_target_pairs={{8,0},{16,8},{24,16},{32,24},{40,32},{48,40},{56,48},{64,56},{72,6... | collective-permute-start | bytes 3145736 | tf_op jit(solution)/shard_map/ppermute | solution.py:16
  144.5 76.6 %collective-permute-start.1 = (bf16[1024,512]{1,0:T(8,128)(2,1)S(1)}, bf16[1024,512]{1,0:T(8,128)(2,1)}, u32[]{:S(2)}, u32[]{:S(2)}) collective-permute-start(bf16[1024,512]{1,0:T(8,128)(2,1)S(1)} %convolution_convert_fusion), channel_id=1, source_target_pairs={{16,0},{24,8},{32,16},{40,24},{48,32},{56,40},{64,48},{72,56},{80,... | collective-permute-start | bytes 3145736 | tf_op jit(solution)/shard_map/ppermute | solution.py:16
  356.0 14.6 %copy-start.2 = (f32[8,512,512]{2,1,0:T(8,128)S(1)}, f32[8,512,512]{2,1,0:T(8,128)}, u32[]{:S(2)}) copy-start(f32[8,512,512]{2,1,0:T(8,128)} %get-tuple-element.255) | copy-start | bytes 25165828
  487.0 8.2 %copy-start.3 = (f32[4,512,512]{2,1,0:T(8,128)S(1)}, f32[4,512,512]{2,1,0:T(8,128)}, u32[]{:S(2)}) copy-start(f32[4,512,512]{2,1,0:T(8,128)} %get-tuple-element.253) | copy-start | bytes 12582916
  487.0 16.9 %copy-start.1 = (bf16[1024,512]{1,0:T(8,128)(2,1)S(1)}, bf16[1024,512]{1,0:T(8,128)(2,1)}, u32[]{:S(2)}) copy-start(bf16[1024,512]{1,0:T(8,128)(2,1)} %param.8) | copy-start | bytes 3145732
Sparse Core Ops, SparseCore 0:
  10.2 121.7 all-gather.4
  133.7 72.9 all-gather.2
  384.4 66.2 reduce-scatter.1
where the time goes:
time: 515 us; the launch traced here: 511 us
  waiting for transfers between devices  176 us (34%)
  other arithmetic  163 us (32%)
  matrix products  107 us (21%)
  local copies, waits for them, and re-layouts  45 us (9%)
  between operations  14.1 us (3%)
    all_gather x1, waiting for transfers between devices, per_device(): lax.all_gather(out_grad, 'chan', axis=1, tiled=True)  123 us
    sub x8, other arithmetic, add_lag(): totals[1] + coef_real * slice_imag - coef_imag * slice_real  74 us
    sub x4, other arithmetic, add_block(): totals[1] + coef_real * slice_imag - coef_imag * slice_real  69.7 us
    all_gather x1, waiting for transfers between devices, per_device(): whole_filter = lax.all_gather(filt, 'seq', axis=0, tiled=True)  51.2 us
    dot_general x3, matrix products, spectrum(): imag_part = -jnp.einsum('fb,nbc->nfc', sin_table, blocks, precision=level)  29.2 us
    dot_general x3, matrix products, spectrum(): real_part = jnp.einsum('fb,nbc->nfc', cos_table, blocks, precision=level)  24.9 us
    unnamed x10, local copies, waits for them, and re-layouts  24.3 us
    dot_general x2, matrix products, inverse(): front = jnp.einsum('fa,nfc->nac', cos_table, real_part, precision=highest)  22.7 us
  transfers between devices with their start and end apart: 5, of which 2 were waited for; matrix products, arithmetic and copies ran while one was open for 30% of the time, Pallas kernels for 0%

commit v1 on v0

--- a/solution.py
+++ b/solution.py
@@ -8,6 +8,12 @@
 BLOCK = 256
 highest = lax.Precision.HIGHEST
 higher = lax.Precision.HIGH
+
+
+def quotas_keep_up(here_x):
+    return jnp.concatenate(
+        lax.all_to_all(jnp.stack(lax.axis_size("chan") * [here_x]), "chan", 0, 0), axis=1
+    )
 
 
 def from_behind(block, axis, distance):
@@ -21,7 +27,7 @@
     block_len = BLOCK
     frame_len = 2 * BLOCK
     mixed_sum = lax.dot_general(
-        lax.all_gather(out_grad, "chan", axis=1, tiled=True),
+        quotas_keep_up(out_grad),
         out_weight,
         (((1,), (1,)), ((), ())),
         preferred_element_type=jnp.float32,

time: 515 us -> 489 us (0.950)
  the two profiles are of different devices: /device:TPU:3 before, /device:TPU:30 now
where the time goes in v1:
time: 489 us; the launch traced here: 483 us
  other arithmetic  163 us (33%)
  waiting for transfers between devices  135 us (28%)
  matrix products  107 us (22%)
  local copies, waits for them, and re-layouts  50.9 us (10%)
  between operations  14.4 us (3%)
  starting transfers between devices  11.3 us (2%)
    all_to_all x1, waiting for transfers between devices, quotas_keep_up(): lax.all_to_all(jnp.stack(lax.axis_size('chan') * [here_x]), 'chan', 0, 0)  123 us
    sub x8, other arithmetic, add_lag(): totals[1] + coef_real * slice_imag - coef_imag * slice_real  74 us
    sub x4, other arithmetic, add_block(): totals[1] + coef_real * slice_imag - coef_imag * slice_real  69.8 us
    dot_general x3, matrix products, spectrum(): imag_part = -jnp.einsum('fb,nbc->nfc', sin_table, blocks, precision=level)  29.3 us
    unnamed x11, local copies, waits for them, and re-layouts  25.9 us
    dot_general x3, matrix products, spectrum(): real_part = jnp.einsum('fb,nbc->nfc', cos_table, blocks, precision=level)  24.9 us
    dot_general x2, matrix products, inverse(): front = jnp.einsum('fa,nfc->nac', cos_table, real_part, precision=highest)  22.7 us
    dot_general x2, matrix products, inverse(): back = jnp.einsum('fa,nfc->nac', sin_table, imag_part, precision=highest)  20.8 us
  transfers between devices with their start and end apart: 5, of which 2 were waited for; matrix products, arithmetic and copies ran while one was open for 31% of the time, Pallas kernels for 0%

profile of v1, /device:TPU:30, one launch (start us, length us, event | category | flops | bytes accessed | tf_op | source)
XLA Modules:
  0.0 482.7 jit_solution(12264850332394792786)
XLA Ops:
  8.8 4.3 stack.2
  13.1 7.2 %all-to-all-start = ((bf16[8,1024,512]{1,2,0:T(8,128)(2,1)}), bf16[8,1024,512]{1,2,0:T(8,128)(2,1)}, u32[]{:S(2)}, u32[]{:S(2)}) async-start(bf16[8,1024,512]{1,2,0:T(8,128)(2,1)} %stack.2), calls=%async_computation | async-start | bytes 16777216 | tf_op jit(solution)/shard_map/all_to_all | solution.py:15
  21.0 123.4 %all-to-all-done = bf16[8,1024,512]{1,2,0:T(8,128)(2,1)} async-done(((bf16[8,1024,512]{1,2,0:T(8,128)(2,1)}), bf16[8,1024,512]{1,2,0:T(8,128)(2,1)}, u32[]{:S(2)}, u32[]{:S(2)}) %all-to-all-start) | async-done | bytes 8388640 | tf_op jit(solution)/shard_map/all_to_all | solution.py:15
  144.4 9.1 %convolution_convert_fusion = bf16[1024,512]{1,0:T(8,128)(2,1)S(1)} fusion(bf16[1024,4096]{0,1:T(8,128)(2,1)} %bitcast.4, bf16[512,4096]{1,0:T(8,128)(2,1)} %param.10), kind=kOutput, calls=%fused_computation.25 | convolution fusion | flops 4295491584 | bytes 13631488 | tf_op jit(solution)/shard_map/dot_general | solution.py:29
  157.7 4.7 convolution_bitcast_fusion.2
  162.4 4.7 negate_bitcast_fusion.2
  167.1 14.5 %convolution_bitcast_fusion.1 = f32[8,512,512]{2,1,0:T(8,128)} fusion(f32[8,256,512]{2,1,0:T(8,128)} %bitcast.80), kind=kOutput, calls=%fused_computation.21 | convolution fusion | flops 6444285952 | bytes 12582912 | tf_op jit(solution)/shard_map/fb,nbc->nfc/dot_general | solution.py:49
  181.6 11.1 %collective-permute-done.1 = bf16[1024,512]{1,0:T(8,128)(2,1)} collective-permute-done((bf16[1024,512]{1,0:T(8,128)(2,1)S(1)}, bf16[1024,512]{1,0:T(8,128)(2,1)}, u32[]{:S(2)}, u32[]{:S(2)}) %collective-permute-start.1) | collective-permute-done | bytes 1048608 | tf_op jit(solution)/shard_map/ppermute | solution.py:22
  194.3 5.7 %convolution_bitcast_fusion = f32[12,512,512]{1,2,0:T(8,128)S(1)} fusion(bf16[12,256,512]{2,1,0:T(8,128)(2,1)S(1)} %bitcast.78), kind=kOutput, calls=%fused_computation.18 | convolution fusion | flops 4833673216 | bytes 15728640 | tf_op jit(solution)/shard_map/fb,nbc->nfc/dot_general | solution.py:49
  200.0 9.9 %negate_bitcast_fusion = f32[12,512,512]{1,2,0:T(8,128)} fusion(bf16[12,256,512]{2,1,0:T(8,128)(2,1)S(1)} %bitcast.79), kind=kOutput, calls=%fused_computation.12 | convolution fusion | flops 4836818944 | bytes 15728640 | tf_op jit(solution)/shard_map/fb,nbc->nfc/dot_general | solution.py:50
  210.0 16.4 %fusion.4 = (f32[11,512,512]{1,2,0:T(8,128)}, f32[11,512,512]{1,2,0:T(8,128)}) fusion(f32[12,512,512]{1,2,0:T(8,128)} %negate_bitcast_fusion, f32[512]{0:T(512)S(1)} %fusion.39, f32[12,512,512]{1,2,0:T(8,128)S(1)} %convolution_bitcast_fusion), kind=kLoop, calls=%fused_computation.14 | loop fusion | flops 11534336 | bytes 69208064 | tf_op jit(solution)/shard_map/add | solution.py:62
  226.3 12.1 %copy.25 = f32[11,512,512]{2,1,0:T(8,128)} copy(f32[11,512,512]{1,2,0:T(8,128)} %get-tuple-element.369) | data formatting | bytes 23068672
  238.5 12.2 %copy.26 = f32[11,512,512]{2,1,0:T(8,128)} copy(f32[11,512,512]{1,2,0:T(8,128)} %get-tuple-element.368) | data formatting | bytes 23068672
  250.6 77.0 %while.33 = (s32[]{:T(128)}, f32[8,512,512]{2,1,0:T(8,128)}, f32[8,512,512]{2,1,0:T(8,128)}, f32[4,512,512]{2,1,0:T(8,128)}, f32[11,512,512]{2,1,0:T(8,128)}, /*...) while((s32[]{:T(128)}, f32[8,512,512]{2,1,0:T(8,128)}, ...), condition=%wide.region_3.4_spmd.clone, body=%wide.region_2.3_spmd.clone.sunk | while | flops 20971524 | bytes 56623212 | solution.py:94
  252.7 11.9 %fusion.96 = (f32[8,512,512]{2,1,0:T(8,128)}, f32[8,512,512]{2,1,0:T(8,128)}) fusion(f32[8,512,512]{2,1,0:T(8,128)} %get-tuple-element.510, f32[11,512,512]{2,1,0:T(8,128)} %get-tuple-element.523, s32[]{:T(128)} %get-tuple-element.508, f32[11,512,512]{2,1,0:T(8,128)} %get-tuple-element.521, f32[512,512]{1,0:T(8,128)S(1)} %get-tuple-element.468, ...), kind=kLoop, calls=%fused_computation.7.clone.1 | loop fusion | flops 20971520 | bytes 52428804 | tf_op jit(solution)/shard_map/while/body/eval_jaxpr/sub | solution.py:90
  266.4 19.3 %fusion.96 = (f32[8,512,512]{2,1,0:T(8,128)}, f32[8,512,512]{2,1,0:T(8,128)}) fusion(f32[8,512,512]{2,1,0:T(8,128)} %get-tuple-element.510, f32[11,512,512]{2,1,0:T(8,128)} %get-tuple-element.523, s32[]{:T(128)} %get-tuple-element.508, f32[11,512,512]{2,1,0:T(8,128)} %get-tuple-element.521, f32[512,512]{1,0:T(8,128)S(1)} %get-tuple-element.468, ...), kind=kLoop, calls=%fused_computation.7.clone.1 | loop fusion | flops 20971520 | bytes 52428804 | tf_op jit(solution)/shard_map/while/body/eval_jaxpr/sub | solution.py:90
  287.4 19.3 %fusion.96 = (f32[8,512,512]{2,1,0:T(8,128)}, f32[8,512,512]{2,1,0:T(8,128)}) fusion(f32[8,512,512]{2,1,0:T(8,128)} %get-tuple-element.510, f32[11,512,512]{2,1,0:T(8,128)} %get-tuple-element.523, s32[]{:T(128)} %get-tuple-element.508, f32[11,512,512]{2,1,0:T(8,128)} %get-tuple-element.521, f32[512,512]{1,0:T(8,128)S(1)} %get-tuple-element.468, ...), kind=kLoop, calls=%fused_computation.7.clone.1 | loop fusion | flops 20971520 | bytes 52428804 | tf_op jit(solution)/shard_map/while/body/eval_jaxpr/sub | solution.py:90
  308.4 19.3 %fusion.96 = (f32[8,512,512]{2,1,0:T(8,128)}, f32[8,512,512]{2,1,0:T(8,128)}) fusion(f32[8,512,512]{2,1,0:T(8,128)} %get-tuple-element.510, f32[11,512,512]{2,1,0:T(8,128)} %get-tuple-element.523, s32[]{:T(128)} %get-tuple-element.508, f32[11,512,512]{2,1,0:T(8,128)} %get-tuple-element.521, f32[512,512]{1,0:T(8,128)S(1)} %get-tuple-element.468, ...), kind=kLoop, calls=%fused_computation.7.clone.1 | loop fusion | flops 20971520 | bytes 52428804 | tf_op jit(solution)/shard_map/while/body/eval_jaxpr/sub | solution.py:90
  327.7 14.5 %fusion.15 = f32[8,512,256]{1,2,0:T(8,128)S(1)} fusion(f32[8,512,512]{2,1,0:T(8,128)} %get-tuple-element.254), kind=kOutput, calls=%fused_computation.38 | convolution fusion | flops 6444285952 | bytes 12582912 | tf_op jit(solution)/shard_map/fa,nfc->nac/dot_general | solution.py:54
  342.2 13.8 %subtract_multiply_fusion = f32[8,512,256]{1,2,0:T(8,128)} fusion(f32[8,512,256]{1,2,0:T(8,128)S(1)} %fusion.15, f32[8,512,512]{2,1,0:T(8,128)S(1)} %copy-done.2), kind=kOutput, calls=%fused_computation.19 | convolution fusion | flops 6446383104 | bytes 16777216 | tf_op jit(solution)/shard_map/fa,nfc->nac/dot_general | solution.py:55
  356.0 14.6 %negate_bitcast_fusion.1 = f32[8,512,512]{2,1,0:T(8,128)} fusion(f32[8,256,512]{2,1,0:T(8,128)} %bitcast.81), kind=kOutput, calls=%fused_computation.17 | convolution fusion | flops 6446383104 | bytes 12582912 | tf_op jit(solution)/shard_map/fb,nbc->nfc/dot_general | solution.py:50
  370.6 88.1 %while.32 = (s32[]{:T(128)}, f32[4,512,512]{2,1,0:T(8,128)}, f32[4,512,512]{2,1,0:T(8,128)}, f32[8,512,512]{2,1,0:T(8,128)}, f32[11,512,512]{2,1,0:T(8,128)}, /*...) while((s32[]{:T(128)}, f32[4,512,512]{2,1,0:T(8,128)}, ...), condition=%wide.region_1.2_spmd.clone, body=%wide.region_0.1_spmd.clone.sunk | while | flops 10485763 | bytes 31457388 | solution.py:81
  372.4 6.9 %fusion.95 = (f32[4,512,512]{2,1,0:T(8,128)}, f32[4,512,512]{2,1,0:T(8,128)}) fusion(f32[4,512,512]{2,1,0:T(8,128)} %get-tuple-element.483, f32[11,512,512]{2,1,0:T(8,128)} %get-tuple-element.496, s32[]{:T(128)} %get-tuple-element.481, f32[11,512,512]{2,1,0:T(8,128)} %get-tuple-element.494, f32[512,512]{1,0:T(8,128)S(1)} %get-tuple-element.457, ...), kind=kLoop, calls=%fused_computation.1.clone.1 | loop fusion | flops 10485760 | bytes 27262980 | tf_op jit(solution)/shard_map/while/body/eval_jaxpr/sub | solution.py:77
  381.0 9.8 %fusion.95 = (f32[4,512,512]{2,1,0:T(8,128)}, f32[4,512,512]{2,1,0:T(8,128)}) fusion(f32[4,512,512]{2,1,0:T(8,128)} %get-tuple-element.483, f32[11,512,512]{2,1,0:T(8,128)} %get-tuple-element.496, s32[]{:T(128)} %get-tuple-element.481, f32[11,512,512]{2,1,0:T(8,128)} %get-tuple-element.494, f32[512,512]{1,0:T(8,128)S(1)} %get-tuple-element.457, ...), kind=kLoop, calls=%fused_computation.1.clone.1 | loop fusion | flops 10485760 | bytes 27262980 | tf_op jit(solution)/shard_map/while/body/eval_jaxpr/sub | solution.py:77
  392.6 9.8 %fusion.95 = (f32[4,512,512]{2,1,0:T(8,128)}, f32[4,512,512]{2,1,0:T(8,128)}) fusion(f32[4,512,512]{2,1,0:T(8,128)} %get-tuple-element.483, f32[11,512,512]{2,1,0:T(8,128)} %get-tuple-element.496, s32[]{:T(128)} %get-tuple-element.481, f32[11,512,512]{2,1,0:T(8,128)} %get-tuple-element.494, f32[512,512]{1,0:T(8,128)S(1)} %get-tuple-element.457, ...), kind=kLoop, calls=%fused_computation.1.clone.1 | loop fusion | flops 10485760 | bytes 27262980 | tf_op jit(solution)/shard_map/while/body/eval_jaxpr/sub | solution.py:77
  404.1 9.7 %fusion.95 = (f32[4,512,512]{2,1,0:T(8,128)}, f32[4,512,512]{2,1,0:T(8,128)}) fusion(f32[4,512,512]{2,1,0:T(8,128)} %get-tuple-element.483, f32[11,512,512]{2,1,0:T(8,128)} %get-tuple-element.496, s32[]{:T(128)} %get-tuple-element.481, f32[11,512,512]{2,1,0:T(8,128)} %get-tuple-element.494, f32[512,512]{1,0:T(8,128)S(1)} %get-tuple-element.457, ...), kind=kLoop, calls=%fused_computation.1.clone.1 | loop fusion | flops 10485760 | bytes 27262980 | tf_op jit(solution)/shard_map/while/body/eval_jaxpr/sub | solution.py:77
  415.5 9.6 %fusion.95 = (f32[4,512,512]{2,1,0:T(8,128)}, f32[4,512,512]{2,1,0:T(8,128)}) fusion(f32[4,512,512]{2,1,0:T(8,128)} %get-tuple-element.483, f32[11,512,512]{2,1,0:T(8,128)} %get-tuple-element.496, s32[]{:T(128)} %get-tuple-element.481, f32[11,512,512]{2,1,0:T(8,128)} %get-tuple-element.494, f32[512,512]{1,0:T(8,128)S(1)} %get-tuple-element.457, ...), kind=kLoop, calls=%fused_computation.1.clone.1 | loop fusion | flops 10485760 | bytes 27262980 | tf_op jit(solution)/shard_map/while/body/eval_jaxpr/sub | solution.py:77
  426.8 9.4 %fusion.95 = (f32[4,512,512]{2,1,0:T(8,128)}, f32[4,512,512]{2,1,0:T(8,128)}) fusion(f32[4,512,512]{2,1,0:T(8,128)} %get-tuple-element.483, f32[11,512,512]{2,1,0:T(8,128)} %get-tuple-element.496, s32[]{:T(128)} %get-tuple-element.481, f32[11,512,512]{2,1,0:T(8,128)} %get-tuple-element.494, f32[512,512]{1,0:T(8,128)S(1)} %get-tuple-element.457, ...), kind=kLoop, calls=%fused_computation.1.clone.1 | loop fusion | flops 10485760 | bytes 27262980 | tf_op jit(solution)/shard_map/while/body/eval_jaxpr/sub | solution.py:77
  438.0 9.4 %fusion.95 = (f32[4,512,512]{2,1,0:T(8,128)}, f32[4,512,512]{2,1,0:T(8,128)}) fusion(f32[4,512,512]{2,1,0:T(8,128)} %get-tuple-element.483, f32[11,512,512]{2,1,0:T(8,128)} %get-tuple-element.496, s32[]{:T(128)} %get-tuple-element.481, f32[11,512,512]{2,1,0:T(8,128)} %get-tuple-element.494, f32[512,512]{1,0:T(8,128)S(1)} %get-tuple-element.457, ...), kind=kLoop, calls=%fused_computation.1.clone.1 | loop fusion | flops 10485760 | bytes 27262980 | tf_op jit(solution)/shard_map/while/body/eval_jaxpr/sub | solution.py:77
  449.1 9.4 %fusion.95 = (f32[4,512,512]{2,1,0:T(8,128)}, f32[4,512,512]{2,1,0:T(8,128)}) fusion(f32[4,512,512]{2,1,0:T(8,128)} %get-tuple-element.483, f32[11,512,512]{2,1,0:T(8,128)} %get-tuple-element.496, s32[]{:T(128)} %get-tuple-element.481, f32[11,512,512]{2,1,0:T(8,128)} %get-tuple-element.494, f32[512,512]{1,0:T(8,128)S(1)} %get-tuple-element.457, ...), kind=kLoop, calls=%fused_computation.1.clone.1 | loop fusion | flops 10485760 | bytes 27262980 | tf_op jit(solution)/shard_map/while/body/eval_jaxpr/sub | solution.py:77
  458.7 8.2 %fusion.17 = f32[4,512,256]{1,2,0:T(8,128)S(1)} fusion(f32[4,512,512]{2,1,0:T(8,128)} %get-tuple-element.252), kind=kOutput, calls=%fused_computation.40 | convolution fusion | flops 3223060480 | bytes 6291456 | tf_op jit(solution)/shard_map/fa,nfc->nac/dot_general | solution.py:54
  466.9 7.0 %multiply_convert_fusion = bf16[4,512,256]{1,2,0:T(8,128)(2,1)} fusion(f32[4,512,256]{1,2,0:T(8,128)S(1)} %fusion.17, f32[4,512,512]{2,1,0:T(8,128)S(1)} %copy-done.3), kind=kOutput, calls=%fused_computation.24 | convolution fusion | flops 3224633344 | bytes 7340032 | tf_op jit(solution)/shard_map/fa,nfc->nac/dot_general | solution.py:55
  (37 shorter events, 30.4 us)
Async XLA Ops:
  7.2 150.5 %copy-start = (bf16[1024,512]{1,0:T(8,128)(2,1)S(1)}, bf16[1024,512]{1,0:T(8,128)(2,1)}, u32[]{:S(2)}) copy-start(bf16[1024,512]{1,0:T(8,128)(2,1)} %param.8) | copy-start | bytes 3145732
  13.1 131.3 %all-to-all-start = ((bf16[8,1024,512]{1,2,0:T(8,128)(2,1)}), bf16[8,1024,512]{1,2,0:T(8,128)(2,1)}, u32[]{:S(2)}, u32[]{:S(2)}) async-start(bf16[8,1024,512]{1,2,0:T(8,128)(2,1)} %stack.2), calls=%async_computation | async-start | bytes 16777216 | tf_op jit(solution)/shard_map/all_to_all | solution.py:15
  20.3 146.9 %all-gather.2.cloned.1.call-start = ((), (), s32[]{:S(2)}) async-start(), calls=%async_computation.2 | async-start | bytes 4456448 | tf_op jit(solution)/shard_map/all_gather | solution.py:36
  21.0 453.0 %reduce-scatter.2.cloned.1.call-start = ((), (), s32[]{:S(2)}) async-start(), calls=%async_computation.3 | async-start | bytes 4456448 | tf_op jit(solution)/shard_map/reduce_scatter | solution.py:99
  153.5 28.1 %collective-permute-start = (bf16[1024,512]{1,0:T(8,128)(2,1)S(1)}, bf16[1024,512]{1,0:T(8,128)(2,1)S(1)}, u32[]{:S(2)}, u32[]{:S(2)}) collective-permute-start(bf16[1024,512]{1,0:T(8,128)(2,1)S(1)} %convolution_convert_fusion), channel_id=1, source_target_pairs={{8,0},{16,8},{24,16},{32,24},{40,32},{48,40},{56,48},{64,56},{72,6... | collective-permute-start | bytes 3145736 | tf_op jit(solution)/shard_map/ppermute | solution.py:22
  155.5 37.3 %collective-permute-start.1 = (bf16[1024,512]{1,0:T(8,128)(2,1)S(1)}, bf16[1024,512]{1,0:T(8,128)(2,1)}, u32[]{:S(2)}, u32[]{:S(2)}) collective-permute-start(bf16[1024,512]{1,0:T(8,128)(2,1)S(1)} %convolution_convert_fusion), channel_id=1, source_target_pairs={{16,0},{24,8},{32,16},{40,24},{48,32},{56,40},{64,48},{72,56},{80,... | collective-permute-start | bytes 3145736 | tf_op jit(solution)/shard_map/ppermute | solution.py:22
  327.7 14.6 %copy-start.2 = (f32[8,512,512]{2,1,0:T(8,128)S(1)}, f32[8,512,512]{2,1,0:T(8,128)}, u32[]{:S(2)}) copy-start(f32[8,512,512]{2,1,0:T(8,128)} %get-tuple-element.255) | copy-start | bytes 25165828
  458.7 8.2 %copy-start.3 = (f32[4,512,512]{2,1,0:T(8,128)S(1)}, f32[4,512,512]{2,1,0:T(8,128)}, u32[]{:S(2)}) copy-start(f32[4,512,512]{2,1,0:T(8,128)} %get-tuple-element.253) | copy-start | bytes 12582916
  458.7 16.9 %copy-start.1 = (bf16[1024,512]{1,0:T(8,128)(2,1)S(1)}, bf16[1024,512]{1,0:T(8,128)(2,1)}, u32[]{:S(2)}) copy-start(bf16[1024,512]{1,0:T(8,128)(2,1)} %param.8) | copy-start | bytes 3145732
Sparse Core Ops, SparseCore 0:
  22.8 106.9 all-gather.1
  356.1 66.6 reduce-scatter.1
